TPU v7x, 512 devices: a whole 4x4x16 slice. The times are simulated.
512 devices in a mesh: row: 32 (over z, x_lo), col: 16 (over y, x_hi, core).
Axes of the slice: x: 4 (x_hi: 2, x_lo: 2; x = x_hi * 2 + x_lo), y: 4, z: 16, core: 2. Of those that a mesh axis runs over, the one named last changes fastest.
Arguments:
- x_window: bfloat16 [3, 2048, 512], P(None, 'row', 'col'), may hold values from -6 to 6
- y_window: float32 [3, 2048], P(None, 'row'), may hold values from -6 to 6
- block_order: int32 [3], replicated, may hold values from 0 to 2, each once
- diag_inverse: bfloat16 [3, 2048, 2048], P(None, 'row'), may hold values from -0.5 to 1.5, as said below
- panel_window: bfloat16 [3, 2048, 2048], P(None, 'row', 'col'), may hold values from -0.078125 to 0.078125
- panel_trail: bfloat16 [4096, 3, 2048], P('row', None, 'col'), may hold values from -0.078125 to 0.078125
- x_trail: bfloat16 [4096, 512], P('row', 'col'), may hold values from -6 to 6
- y_trail: float32 [4096], P('row'), may hold values from -6 to 6
Outputs:
- whitened: bfloat16 [3, 2048, 512], P(None, 'row', 'col')
- white_resp: bfloat16 [3, 2048], P(None, 'row')
- trail_rhs: float32 [4096, 512], P('row', 'col')
- trail_resp: float32 [4096], P('row')
- normal_part: float32 [512, 512], P('row')
- right_part: float32 [512], P('row')
Inputs may be any that keep to these rules, and one draw needn't show every extreme that they name: Each diag_inverse[s] is lower triangular with a positive diagonal.
All inputs are finite; a program needn't handle non-finite values.
Results may differ from a plain program's by a relative error of at most 0.014.
Values may be sent and summed in bfloat16 or wider, within the bound.
A program may use at most 64 MiB of HBM per device.

v0:
```python
import jax
import jax.numpy as jnp
from jax import lax
from jax.sharding import PartitionSpec as P


def shards(
    x_window, y_window, block_order, diag_inverse, panel_window, panel_trail, x_trail, y_trail
):
    steps = x_window.shape[0]
    own_rows = x_window.shape[1]
    own_cols = x_window.shape[2]
    width = panel_window.shape[2]
    block_rows = own_rows * lax.axis_size("row")
    full_cols = own_cols * lax.axis_size("col")
    normal_rows = full_cols // lax.axis_size("row")
    col_start = lax.axis_index("col") * width
    normal_start = lax.axis_index("row") * normal_rows
    trail_rows = x_trail.shape[0]
    solved_cols = []
    solved_resp = []
    out_tiles = []
    out_resp = []
    trail_total = jnp.zeros((trail_rows, full_cols), jnp.float32)
    trail_resp_total = jnp.zeros((trail_rows,), jnp.float32)
    gram = jnp.zeros((normal_rows, full_cols), jnp.float32)
    right = jnp.zeros((normal_rows,), jnp.float32)
    for s in range(steps):
        stored = block_order[s]
        pending = lax.dynamic_index_in_dim(x_window, stored, 0, keepdims=False).astype(jnp.float32)
        pending_resp = lax.dynamic_index_in_dim(y_window, stored, 0, keepdims=False)
        if s > 0:
            first = s * (s - 1) // 2
            factors = panel_window[first : first + s]
            earlier = jnp.stack(solved_cols)
            earlier_resp = jnp.stack(solved_resp)
            update = jnp.einsum("trw,twp->rp", factors, earlier, preferred_element_type=jnp.float32)
            update_resp = jnp.einsum(
                "trw,tw->r", factors, earlier_resp, preferred_element_type=jnp.float32
            )
            pending = pending - lax.psum_scatter(update, "col", scatter_dimension=1, tiled=True)
            pending_resp = pending_resp - lax.psum(update_resp, "col")
        residual = pending.astype(jnp.bfloat16)
        resid_resp = pending_resp.astype(jnp.bfloat16)
        whole, whole_resp = (
            lax.all_gather(residual, "row", axis=0, tiled=True),
            lax.all_gather(resid_resp, "row", axis=0, tiled=True),
        )
        inverse = diag_inverse[s]
        tile = jnp.dot(inverse, whole, preferred_element_type=jnp.float32).astype(jnp.bfloat16)
        tile_resp = jnp.dot(inverse, whole_resp, preferred_element_type=jnp.float32).astype(
            jnp.bfloat16
        )
        out_tiles.append(tile)
        out_resp.append(tile_resp)
        all_rows, all_resp = (
            lax.all_gather(tile, "row", axis=0, tiled=True),
            lax.all_gather(tile_resp, "row", axis=0, tiled=True),
        )
        mine = lax.all_to_all(all_rows, "col", split_axis=0, concat_axis=1, tiled=True)
        mine_resp = lax.dynamic_slice_in_dim(all_resp, col_start, width, 0)
        solved_cols.append(mine)
        solved_resp.append(mine_resp)
        factor_rows = panel_trail[:, s, :]
        trail_total = trail_total + jnp.dot(factor_rows, mine, preferred_element_type=jnp.float32)
        trail_resp_total = trail_resp_total + jnp.dot(
            factor_rows, mine_resp, preferred_element_type=jnp.float32
        )
        slab = lax.dynamic_slice_in_dim(mine, normal_start, normal_rows, 1)
        gram = gram + lax.dot_general(
            slab, mine, (((0,), (0,)), ((), ())), preferred_element_type=jnp.float32
        )
        right = right + lax.dot_general(
            slab, mine_resp, (((0,), (0,)), ((), ())), preferred_element_type=jnp.float32
        )
    summed = lax.psum(trail_total.astype(jnp.bfloat16), "col").astype(jnp.float32)
    share = lax.dynamic_slice_in_dim(summed, lax.axis_index("col") * own_cols, own_cols, 1)
    trail_rhs = x_trail.astype(jnp.float32) - share
    gram, right, resp_sum = lax.psum((gram, right, trail_resp_total), "col")
    trail_resp = y_trail - resp_sum
    scale = 1.0 / (steps * block_rows)
    whitened = jnp.stack(out_tiles)
    white_resp = jnp.stack(out_resp)
    return (whitened, white_resp, trail_rhs, trail_resp, gram * scale, right * scale)


def solution(mesh):
    in_specs = (
        P(None, "row", "col"),
        P(None, "row"),
        P(),
        P(None, "row", None),
        P(None, "row", "col"),
        P("row", None, "col"),
        P("row", "col"),
        P("row"),
    )
    out_specs = (
        P(None, "row", "col"),
        P(None, "row"),
        P("row", "col"),
        P("row"),
        P("row", None),
        P("row"),
    )
    return jax.shard_map(shards, mesh=mesh, in_specs=in_specs, out_specs=out_specs, check_vma=False)
```

profile of v0, /device:TPU:1, one launch (start us, length us, event | category | flops | bytes accessed | tf_op | source)
XLA Modules:
  0.0 1263.4 jit_solution(17524989272356092082)
XLA Ops:
  7.2 1.4 fusion.84
  14.5 61.7 %all-gather = bf16[1,2048,32]{2,0,1:T(2,128)(2,1)S(1)} all-gather(bf16[1,64,32]{2,0,1:T(2,128)(2,1)S(1)} %copy.62), channel_id=2, replica_groups=mesh['row'=32,'col'=16] {'row'}, dimensions={1}, use_global_device_ids=true | all-gather | bytes 135168 | tf_op jit(solution)/shard_map/all_gather | solution.py:46
  76.2 0.5 copy.42
  76.8 0.6 copy-done
  77.4 0.2 fusion.2
  77.5 46.4 %all-gather.2 = bf16[32,64,32]{1,2,0:T(8,128)(2,1)S(1)} all-gather(bf16[1,64,32]{1,2,0:T(8,128)(2,1)S(1)} %fusion.2), channel_id=1, replica_groups=mesh['row'=32,'col'=16] {'row'}, dimensions={0}, use_global_device_ids=true | all-gather | bytes 135168 | tf_op jit(solution)/shard_map/all_gather | solution.py:57
  124.2 0.7 copy.45
  124.9 34.9 %all-to-all-start = ((bf16[16,128,32]{1,2,0:T(8,128)(2,1)}), bf16[16,128,32]{1,2,0:T(8,128)(2,1)S(1)}, u32[]{:S(2)}, u32[]{:S(2)}) async-start(bf16[16,128,32]{1,2,0:T(8,128)(2,1)} %copy.45), calls=%async_computation | async-start | bytes 262144 | tf_op jit(solution)/shard_map/all_to_all | solution.py:60
  159.9 0.6 copy-done.5
  160.5 1.3 dynamic-slice
  162.4 0.2 dynamic-update-slice
  162.7 47.3 %all-reduce = bf16[2048]{0:T(1024)(128)(2,1)S(1)} all-reduce(bf16[2048]{0:T(1024)(128)(2,1)S(1)} %dynamic-update-slice), channel_id=3, replica_groups=mesh['row'=32,'col'=16] {'row'}, use_global_device_ids=true, to_apply=%add | all-reduce | flops 2048 | bytes 8192 | tf_op jit(solution)/shard_map/all_gather | solution.py:47
  210.2 0.2 dynamic-update-slice.1
  210.4 46.7 %all-reduce.1 = bf16[2048]{0:T(1024)(128)(2,1)S(1)} all-reduce(bf16[2048]{0:T(1024)(128)(2,1)S(1)} %dynamic-update-slice.1), channel_id=1, replica_groups=mesh['row'=32,'col'=16] {'row'}, use_global_device_ids=true, to_apply=%add.1 | all-reduce | flops 2048 | bytes 8192
  257.2 0.2 convolution_bitcast_fusion.9
  257.4 60.9 %psum.42 = f32[64]{0:T(128)S(1)} all-reduce(f32[64]{0:T(128)S(1)} %convolution_bitcast_fusion.9), channel_id=1, replica_groups=mesh['row'=32,'col'=16] {'col'}, use_global_device_ids=true, to_apply=%region_2.3 | all-reduce | flops 64 | bytes 512 | tf_op jit(solution)/shard_map/psum | solution.py:42
  318.3 0.2 dynamic-update-slice.2
  318.5 47.1 %all-reduce.2 = bf16[2048]{0:T(1024)(128)(2,1)S(1)} all-reduce(bf16[2048]{0:T(1024)(128)(2,1)S(1)} %dynamic-update-slice.2), channel_id=1, replica_groups=mesh['row'=32,'col'=16] {'row'}, use_global_device_ids=true, to_apply=%add.2 | all-reduce | flops 2048 | bytes 8192
  365.8 0.2 dynamic-update-slice.3
  366.0 47.2 %all-reduce.3 = bf16[2048]{0:T(1024)(128)(2,1)S(1)} all-reduce(bf16[2048]{0:T(1024)(128)(2,1)S(1)} %dynamic-update-slice.3), channel_id=1, replica_groups=mesh['row'=32,'col'=16] {'row'}, use_global_device_ids=true, to_apply=%add.3 | all-reduce | flops 2048 | bytes 8192
  413.4 60.5 %psum.43 = f32[64]{0:T(128)S(1)} all-reduce(f32[64]{0:T(128)S(1)} %convolution_bitcast_fusion.2), channel_id=1, replica_groups=mesh['row'=32,'col'=16] {'col'}, use_global_device_ids=true, to_apply=%region_3.4 | all-reduce | flops 64 | bytes 512 | tf_op jit(solution)/shard_map/psum | solution.py:42
  473.9 0.2 dynamic-update-slice.4
  474.2 47.3 %all-reduce.4 = bf16[2048]{0:T(1024)(128)(2,1)S(1)} all-reduce(bf16[2048]{0:T(1024)(128)(2,1)S(1)} %dynamic-update-slice.4), channel_id=1, replica_groups=mesh['row'=32,'col'=16] {'row'}, use_global_device_ids=true, to_apply=%add.4 | all-reduce | flops 2048 | bytes 8192
  521.6 0.2 fusion.9
  521.7 0.2 dynamic-update-slice.5
  521.9 46.9 %all-reduce.5 = bf16[2048]{0:T(1024)(128)(2,1)S(1)} all-reduce(bf16[2048]{0:T(1024)(128)(2,1)S(1)} %dynamic-update-slice.5), channel_id=1, replica_groups=mesh['row'=32,'col'=16] {'row'}, use_global_device_ids=true, to_apply=%add.5 | all-reduce | flops 2048 | bytes 8192
  568.9 0.2 convolution_bitcast_fusion.8
  569.0 0.2 fusion.8
  569.2 0.2 fusion.7
  569.6 0.6 pad_maximum_fusion.1
  570.4 0.2 convolution_bitcast_fusion.5
  570.6 0.8 copy.58
  571.6 0.2 fusion.35
  571.7 105.4 %reduce-scatter.7.cloned.1.call-done = f32[32,64]{1,0:T(8,128)} async-done(((f32[512,64]{1,0:T(8,128)}), f32[32,64]{1,0:T(8,128)}) %reduce-scatter.7.cloned.1.call-update) | async-done | bytes 8208
  677.1 0.8 copy.59
  678.0 50.2 %all-gather.3 = bf16[32,64,32]{1,2,0:T(8,128)(2,1)S(1)} all-gather(bf16[1,64,32]{1,2,0:T(8,128)(2,1)S(1)} %copy.46), channel_id=1, replica_groups=mesh['row'=32,'col'=16] {'row'}, dimensions={0}, use_global_device_ids=true | all-gather | bytes 135168 | tf_op jit(solution)/shard_map/all_gather | solution.py:46
  728.3 0.3 reshape.65
  728.6 0.2 fusion.3
  728.7 46.4 %all-gather.4 = bf16[32,64,32]{1,2,0:T(8,128)(2,1)S(1)} all-gather(bf16[1,64,32]{1,2,0:T(8,128)(2,1)S(1)} %fusion.3), channel_id=1, replica_groups=mesh['row'=32,'col'=16] {'row'}, dimensions={0}, use_global_device_ids=true | all-gather | bytes 135168 | tf_op jit(solution)/shard_map/all_gather | solution.py:57
  775.4 0.7 copy.50
  776.1 34.8 %all-to-all-start.1 = ((bf16[16,128,32]{1,2,0:T(8,128)(2,1)}), bf16[16,128,32]{1,2,0:T(8,128)(2,1)S(1)}, u32[]{:S(2)}, u32[]{:S(2)}) async-start(bf16[16,128,32]{1,2,0:T(8,128)(2,1)} %copy.50), calls=%async_computation.1 | async-start | bytes 262144 | tf_op jit(solution)/shard_map/all_to_all | solution.py:60
  811.0 7.5 all-to-all-done.1
  818.8 0.8 copy.60
  819.6 0.2 convolution_add_fusion.1
  820.0 81.2 %reduce-scatter.9.cloned.1.call-done = f32[32,64]{1,0:T(8,128)} async-done(((f32[512,64]{1,0:T(8,128)}), f32[32,64]{1,0:T(8,128)}) %reduce-scatter.9.cloned.1.call-update) | async-done | bytes 8208
  901.2 0.8 copy.61
  902.1 50.2 %all-gather.5 = bf16[32,64,32]{1,2,0:T(8,128)(2,1)S(1)} all-gather(bf16[1,64,32]{1,2,0:T(8,128)(2,1)S(1)} %copy.53), channel_id=1, replica_groups=mesh['row'=32,'col'=16] {'row'}, dimensions={0}, use_global_device_ids=true | all-gather | bytes 135168 | tf_op jit(solution)/shard_map/all_gather | solution.py:46
  952.3 0.3 reshape.69
  952.6 0.2 fusion.4
  952.8 46.4 %all-gather.6 = bf16[32,64,32]{1,2,0:T(8,128)(2,1)S(1)} all-gather(bf16[1,64,32]{1,2,0:T(8,128)(2,1)S(1)} %fusion.4), channel_id=1, replica_groups=mesh['row'=32,'col'=16] {'row'}, dimensions={0}, use_global_device_ids=true | all-gather | bytes 135168 | tf_op jit(solution)/shard_map/all_gather | solution.py:57
  999.5 0.7 copy.56
  1000.1 34.8 %all-to-all-start.2 = ((bf16[16,128,32]{1,2,0:T(8,128)(2,1)}), bf16[16,128,32]{1,2,0:T(8,128)(2,1)S(1)}, u32[]{:S(2)}, u32[]{:S(2)}) async-start(bf16[16,128,32]{1,2,0:T(8,128)(2,1)} %copy.56), calls=%async_computation.2 | async-start | bytes 262144 | tf_op jit(solution)/shard_map/all_to_all | solution.py:60
  1035.0 0.2 fusion.6
  1035.1 0.6 pad_maximum_fusion
  1035.8 6.8 all-to-all-done.2
  1042.6 0.2 fusion.5
  1042.9 60.2 %all-reduce.6 = (f32[128]{0:T(128)S(1)}, f32[16,512]{1,0:T(8,128)S(1)}, f32[16]{0:T(128)S(1)}) all-reduce(f32[128]{0:T(128)S(1)} %fusion.7, f32[16,512]{1,0:T(8,128)S(1)} %convolution_add_fusion.2, f32[16]{0:T(128)S(1)} %fusion.5), channel_id=1, replica_groups=mesh['row'=32,'col'=16] {'col'}, use_global_device_ids=true, to_apply=%region_5.6 | all-reduce | flops 8336 | bytes 66688 | tf_op jit(solution)/shard_map/psum | solution.py:79
  1103.1 0.6 broadcast_multiply_fusion
  1103.7 0.8 fusion.1
  1104.6 0.6 copy-done.6
  1105.3 0.5 sub.23
  1105.8 0.5 broadcast_multiply_fusion.1
  1106.3 149.3 %all-reduce.9.cloned.1.call-done = bf16[128,512]{0,1:T(8,128)(2,1)} async-done(((bf16[128,512]{0,1:T(8,128)(2,1)}), bf16[128,512]{0,1:T(8,128)(2,1)}) %all-reduce.9.cloned.1.call-update) | async-done | bytes 131088 | tf_op jit(solution)/shard_map/psum | solution.py:76
  1255.6 1.3 convert_subtract_fusion.2
  (59 shorter events, 3.3 us)
Async XLA Ops:
  7.2 7.2 copy-start.3
  76.2 1.1 copy-start
  124.9 445.3 %all-to-all-start = ((bf16[16,128,32]{1,2,0:T(8,128)(2,1)}), bf16[16,128,32]{1,2,0:T(8,128)(2,1)S(1)}, u32[]{:S(2)}, u32[]{:S(2)}) async-start(bf16[16,128,32]{1,2,0:T(8,128)(2,1)} %copy.45), calls=%async_computation | async-start | bytes 262144 | tf_op jit(solution)/shard_map/all_to_all | solution.py:60
  159.8 0.7 copy-start.5
  159.8 517.3 %reduce-scatter.7.cloned.1.call-start = ((), (), s32[]{:S(2)}) async-start(), calls=%async_computation.6 | async-start | bytes 278528
  210.0 47.2 %copy-start.2 = (bf16[3,64,128]{2,1,0:T(8,128)(2,1)S(1)}, bf16[3,64,128]{2,1,0:T(8,128)(2,1)}, u32[]{:S(2)}) copy-start(bf16[3,64,128]{2,1,0:T(8,128)(2,1)} %param.12) | copy-start | bytes 147460
  521.6 47.3 %copy-start.1 = (bf16[128,3,128]{2,0,1:T(8,128)(2,1)S(1)}, bf16[128,3,128]{2,0,1:T(8,128)(2,1)}, u32[]{:S(2)}) copy-start(bf16[128,3,128]{2,0,1:T(8,128)(2,1)} %param.13) | copy-start | bytes 294916
  776.1 42.4 %all-to-all-start.1 = ((bf16[16,128,32]{1,2,0:T(8,128)(2,1)}), bf16[16,128,32]{1,2,0:T(8,128)(2,1)S(1)}, u32[]{:S(2)}, u32[]{:S(2)}) async-start(bf16[16,128,32]{1,2,0:T(8,128)(2,1)} %copy.50), calls=%async_computation.1 | async-start | bytes 262144 | tf_op jit(solution)/shard_map/all_to_all | solution.py:60
  810.8 90.3 %reduce-scatter.9.cloned.1.call-start = ((), (), s32[]{:S(2)}) async-start(), calls=%async_computation.7 | async-start | bytes 278528
  1000.1 42.4 %all-to-all-start.2 = ((bf16[16,128,32]{1,2,0:T(8,128)(2,1)}), bf16[16,128,32]{1,2,0:T(8,128)(2,1)S(1)}, u32[]{:S(2)}, u32[]{:S(2)}) async-start(bf16[16,128,32]{1,2,0:T(8,128)(2,1)} %copy.56), calls=%async_computation.2 | async-start | bytes 262144 | tf_op jit(solution)/shard_map/all_to_all | solution.py:60
  1034.9 220.7 %all-reduce.9.cloned.1.call-start = ((), (), s32[]{:S(2)}) async-start(), calls=%async_computation.5 | async-start | bytes 262144 | tf_op jit(solution)/shard_map/psum | solution.py:76
  1104.6 151.0 %copy-start.4 = (bf16[128,32]{0,1:T(8,128)(2,1)S(1)}, bf16[128,32]{0,1:T(8,128)(2,1)}, u32[]{:S(2)}) copy-start(bf16[128,32]{0,1:T(8,128)(2,1)} %param.14) | copy-start | bytes 24580
  1104.6 0.7 copy-start.6
Sparse Core Ops, SparseCore 0:
  571.6 105.5 reduce-scatter.6
  819.8 81.3 reduce-scatter.8
  1104.7 150.7 all-reduce.8
where the time goes:
time: 1260 us
  blocking collectives  765 us (61%)
  waiting for transfers between devices  350 us (28%)
  starting transfers between devices  105 us (8%)
  between operations  20.4 us (2%)
  local copies, waits for them, and re-layouts  14.1 us (1%)
    unnamed x5, blocking collectives  235 us
    unnamed x5, waiting for transfers between devices  187 us
    all_gather x3, blocking collectives, shards(): lax.all_gather(residual, 'row', axis=0, tiled=True)  162 us
    psum x1, waiting for transfers between devices, shards(): lax.psum(trail_total.astype(jnp.bfloat16), 'col').astype(jnp.float32)  149 us
    all_gather x3, blocking collectives, shards(): lax.all_gather(tile, 'row', axis=0, tiled=True)  139 us
    psum x2, blocking collectives, shards(): pending_resp = pending_resp - lax.psum(update_resp, 'col')  121 us
    all_to_all x3, starting transfers between devices, shards(): lax.all_to_all(all_rows, 'col', split_axis=0, concat_axis=1, tiled=True)  104 us
    psum x1, blocking collectives, shards(): gram, right, resp_sum = lax.psum((gram, right, trail_resp_total), 'col')  60.2 us
  transfers between devices with their start and end apart: 6, of which 5 were waited for; matrix products, arithmetic and copies ran while one was open for 1% of the time, Pallas kernels for 0%

commit v1 on v0

--- a/solution.py
+++ b/solution.py
@@ -53,8 +53,14 @@
         )
         out_tiles.append(tile)
         out_resp.append(tile_resp)
+
+        def attach_quotas_in(point):
+            extra = lax.axis_size("row")
+            finding = lax.all_to_all(jnp.stack([point] * extra, axis=0), "row", 0, 0)
+            return jnp.concatenate(finding, axis=0)
+
         all_rows, all_resp = (
-            lax.all_gather(tile, "row", axis=0, tiled=True),
+            attach_quotas_in(tile),
             lax.all_gather(tile_resp, "row", axis=0, tiled=True),
         )
         mine = lax.all_to_all(all_rows, "col", split_axis=0, concat_axis=1, tiled=True)

time: 1260 us -> 1070 us (0.85)
  blocking collectives: 765 us -> 620 us
  waiting for transfers between devices: 350 us -> 288 us
    all_gather x3 -> x0, blocking collectives: 139 us -> none  [shards(): lax.all_gather(tile, 'row', axis=0, tiled=True)]
    unnamed x5, waiting for transfers between devices: 187 us -> 119 us
    all_to_all x0 -> x3, starting transfers between devices: none -> 26.5 us  [attach_quotas_in(): finding = lax.all_to_all(jnp.stack([point] * extra, axis=0), 'row', 0, 0)]
    all_to_all x3, starting transfers between devices: 104 us -> 88.2 us  [shards(): lax.all_to_all(all_rows, 'col', split_axis=0, concat_axis=1, tiled=True)]
    psum x2, blocking collectives: 121 us -> 107 us  [shards(): pending_resp = pending_resp - lax.psum(update_resp, 'col')]
    all_to_all x0 -> x3, waiting for transfers between devices: none -> 13.1 us  [attach_quotas_in(): finding = lax.all_to_all(jnp.stack([point] * extra, axis=0), 'row', 0, 0)]
  transfers between devices with their start and end apart: 6 -> 9, of which waited for: 5 -> 6; matrix products, arithmetic and copies ran while one was open for 1% -> 1% of each run, Pallas kernels for 0% -> 0%
where the time goes in v1:
time: 1070 us
  blocking collectives  620 us (58%)
  waiting for transfers between devices  288 us (27%)
  starting transfers between devices  115 us (11%)
  between operations  20.5 us (2%)
  local copies, waits for them, and re-layouts  17.5 us (2%)
    unnamed x5, blocking collectives  239 us
    all_gather x3, blocking collectives, shards(): lax.all_gather(residual, 'row', axis=0, tiled=True)  162 us
    psum x1, waiting for transfers between devices, shards(): lax.psum(trail_total.astype(jnp.bfloat16), 'col').astype(jnp.float32)  142 us
    unnamed x5, waiting for transfers between devices  119 us
    psum x2, blocking collectives, shards(): pending_resp = pending_resp - lax.psum(update_resp, 'col')  107 us
    all_to_all x3, starting transfers between devices, shards(): lax.all_to_all(all_rows, 'col', split_axis=0, concat_axis=1, tiled=True)  88.2 us
    psum x1, blocking collectives, shards(): gram, right, resp_sum = lax.psum((gram, right, trail_resp_total), 'col')  60.2 us
    all_gather x1, blocking collectives, shards(): lax.all_gather(resid_resp, 'row', axis=0, tiled=True)  50.5 us
  transfers between devices with their start and end apart: 9, of which 6 were waited for; matrix products, arithmetic and copies ran while one was open for 1% of the time, Pallas kernels for 0%

profile of v1, /device:TPU:1, one launch (start us, length us, event | category | flops | bytes accessed | tf_op | source)
XLA Modules:
  0.0 1069.5 jit_solution(14413445179035576693)
XLA Ops:
  7.2 1.4 fusion.81
  14.5 61.7 %all-gather = bf16[1,2048,32]{2,0,1:T(2,128)(2,1)S(1)} all-gather(bf16[1,64,32]{2,0,1:T(2,128)(2,1)S(1)} %copy.71), channel_id=2, replica_groups=mesh['row'=32,'col'=16] {'row'}, dimensions={1}, use_global_device_ids=true | all-gather | bytes 135168 | tf_op jit(solution)/shard_map/all_gather | solution.py:46
  76.2 0.5 copy.51
  76.8 0.6 copy-done.5
  77.6 0.8 reshape.118
  78.4 7.3 all-to-all-start
  85.7 0.7 copy-done.4
  86.4 1.3 dynamic-slice
  88.3 0.2 dynamic-update-slice
  88.6 50.5 %all-reduce = bf16[2048]{0:T(1024)(128)(2,1)S(1)} all-reduce(bf16[2048]{0:T(1024)(128)(2,1)S(1)} %dynamic-update-slice), channel_id=3, replica_groups=mesh['row'=32,'col'=16] {'row'}, use_global_device_ids=true, to_apply=%add | all-reduce | flops 2048 | bytes 8192 | tf_op jit(solution)/shard_map/all_gather | solution.py:47
  139.3 0.2 dynamic-update-slice.1
  139.5 46.4 %all-reduce.1 = bf16[2048]{0:T(1024)(128)(2,1)S(1)} all-reduce(bf16[2048]{0:T(1024)(128)(2,1)S(1)} %dynamic-update-slice.1), channel_id=1, replica_groups=mesh['row'=32,'col'=16] {'row'}, use_global_device_ids=true, to_apply=%add.1 | all-reduce | flops 2048 | bytes 8192
  186.1 74.1 %psum.42 = f32[64]{0:T(128)S(1)} all-reduce(f32[64]{0:T(128)S(1)} %convolution_bitcast_fusion.9), channel_id=1, replica_groups=mesh['row'=32,'col'=16] {'col'}, use_global_device_ids=true, to_apply=%region_2.3 | all-reduce | flops 64 | bytes 512 | tf_op jit(solution)/shard_map/psum | solution.py:42
  260.2 0.2 dynamic-update-slice.2
  260.5 47.5 %all-reduce.2 = bf16[2048]{0:T(1024)(128)(2,1)S(1)} all-reduce(bf16[2048]{0:T(1024)(128)(2,1)S(1)} %dynamic-update-slice.2), channel_id=1, replica_groups=mesh['row'=32,'col'=16] {'row'}, use_global_device_ids=true, to_apply=%add.2 | all-reduce | flops 2048 | bytes 8192
  308.1 0.2 dynamic-update-slice.3
  308.3 47.3 %all-reduce.3 = bf16[2048]{0:T(1024)(128)(2,1)S(1)} all-reduce(bf16[2048]{0:T(1024)(128)(2,1)S(1)} %dynamic-update-slice.3), channel_id=1, replica_groups=mesh['row'=32,'col'=16] {'row'}, use_global_device_ids=true, to_apply=%add.3 | all-reduce | flops 2048 | bytes 8192
  355.8 0.2 reshape.119
  356.3 0.7 copy.54
  357.0 30.7 %all-to-all-start.1 = ((bf16[16,128,32]{1,2,0:T(8,128)(2,1)}), bf16[16,128,32]{1,2,0:T(8,128)(2,1)S(1)}, u32[]{:S(2)}, u32[]{:S(2)}) async-start(bf16[16,128,32]{1,2,0:T(8,128)(2,1)} %copy.54), calls=%async_computation.1 | async-start | bytes 262144 | tf_op jit(solution)/shard_map/all_to_all | solution.py:66
  388.0 33.0 %psum.43 = f32[64]{0:T(128)S(1)} all-reduce(f32[64]{0:T(128)S(1)} %convolution_bitcast_fusion.2), channel_id=1, replica_groups=mesh['row'=32,'col'=16] {'col'}, use_global_device_ids=true, to_apply=%region_3.4 | all-reduce | flops 64 | bytes 512 | tf_op jit(solution)/shard_map/psum | solution.py:42
  421.1 0.8 copy.67
  422.0 0.2 dynamic-update-slice.4
  422.3 47.8 %all-reduce.4 = bf16[2048]{0:T(1024)(128)(2,1)S(1)} all-reduce(bf16[2048]{0:T(1024)(128)(2,1)S(1)} %dynamic-update-slice.4), channel_id=1, replica_groups=mesh['row'=32,'col'=16] {'row'}, use_global_device_ids=true, to_apply=%add.4 | all-reduce | flops 2048 | bytes 8192
  470.0 38.3 %reduce-scatter.7.cloned.1.call-done = f32[32,64]{1,0:T(8,128)} async-done(((f32[512,64]{1,0:T(8,128)}), f32[32,64]{1,0:T(8,128)}) %reduce-scatter.7.cloned.1.call-update) | async-done | bytes 8208
  508.4 0.8 copy.68
  509.3 50.2 %all-gather.2 = bf16[32,64,32]{1,2,0:T(8,128)(2,1)S(1)} all-gather(bf16[1,64,32]{1,2,0:T(8,128)(2,1)S(1)} %copy.55), channel_id=1, replica_groups=mesh['row'=32,'col'=16] {'row'}, dimensions={0}, use_global_device_ids=true | all-gather | bytes 135168 | tf_op jit(solution)/shard_map/all_gather | solution.py:46
  559.5 0.3 reshape.75
  559.8 0.2 convolution_convert_fusion.1
  560.1 0.8 reshape.120
  560.9 9.8 all-to-all-start.2
  570.9 0.2 dynamic-update-slice.5
  571.1 50.5 %all-reduce.5 = bf16[2048]{0:T(1024)(128)(2,1)S(1)} all-reduce(bf16[2048]{0:T(1024)(128)(2,1)S(1)} %dynamic-update-slice.5), channel_id=1, replica_groups=mesh['row'=32,'col'=16] {'row'}, use_global_device_ids=true, to_apply=%add.5 | all-reduce | flops 2048 | bytes 8192
  621.9 0.2 reshape.121
  622.4 0.7 copy.59
  623.1 34.9 %all-to-all-start.3 = ((bf16[16,128,32]{1,2,0:T(8,128)(2,1)}), bf16[16,128,32]{1,2,0:T(8,128)(2,1)S(1)}, u32[]{:S(2)}, u32[]{:S(2)}) async-start(bf16[16,128,32]{1,2,0:T(8,128)(2,1)} %copy.59), calls=%async_computation.3 | async-start | bytes 262144 | tf_op jit(solution)/shard_map/all_to_all | solution.py:66
  658.4 0.6 pad_maximum_fusion.1
  659.1 6.6 all-to-all-done.3
  666.0 0.8 copy.69
  667.0 81.0 %reduce-scatter.9.cloned.1.call-done = f32[32,64]{1,0:T(8,128)} async-done(((f32[512,64]{1,0:T(8,128)}), f32[32,64]{1,0:T(8,128)}) %reduce-scatter.9.cloned.1.call-update) | async-done | bytes 8208
  748.0 0.8 copy.70
  748.9 50.5 %all-gather.3 = bf16[32,64,32]{1,2,0:T(8,128)(2,1)S(1)} all-gather(bf16[1,64,32]{1,2,0:T(8,128)(2,1)S(1)} %copy.62), channel_id=1, replica_groups=mesh['row'=32,'col'=16] {'row'}, dimensions={0}, use_global_device_ids=true | all-gather | bytes 135168 | tf_op jit(solution)/shard_map/all_gather | solution.py:46
  799.5 0.3 reshape.77
  799.8 0.2 convolution_convert_fusion
  800.1 0.8 reshape.122
  800.9 9.4 all-to-all-start.4
  810.5 0.2 convolution_bitcast_fusion.5
  810.8 0.2 convolution_add_fusion.1
  811.0 13.1 %all-to-all-done.4 = bf16[32,2,1024]{2,1,0:T(2,128)(2,1)S(1)} async-done(((bf16[32,2,1024]{2,1,0:T(2,128)(2,1)}), bf16[32,2,1024]{2,1,0:T(2,128)(2,1)S(1)}, u32[]{:S(2)}, u32[]{:S(2)}) %all-to-all-start.4) | async-done | bytes 131104 | tf_op jit(solution)/shard_map/all_to_all | solution.py:59
  824.1 0.2 reshape.123
  824.6 0.7 copy.65
  825.3 22.6 %all-to-all-start.5 = ((bf16[16,128,32]{1,2,0:T(8,128)(2,1)}), bf16[16,128,32]{1,2,0:T(8,128)(2,1)S(1)}, u32[]{:S(2)}, u32[]{:S(2)}) async-start(bf16[16,128,32]{1,2,0:T(8,128)(2,1)} %copy.65), calls=%async_computation.5 | async-start | bytes 262144 | tf_op jit(solution)/shard_map/all_to_all | solution.py:66
  847.9 0.2 fusion.3
  848.1 0.6 pad_maximum_fusion
  848.7 6.8 all-to-all-done.5
  855.5 0.2 fusion.2
  855.8 60.2 %all-reduce.6 = (f32[128]{0:T(128)S(1)}, f32[16,512]{1,0:T(8,128)S(1)}, f32[16]{0:T(128)S(1)}) all-reduce(f32[128]{0:T(128)S(1)} %fusion.4, f32[16,512]{1,0:T(8,128)S(1)} %convolution_add_fusion.2, f32[16]{0:T(128)S(1)} %fusion.2), channel_id=1, replica_groups=mesh['row'=32,'col'=16] {'col'}, use_global_device_ids=true, to_apply=%region_5.6 | all-reduce | flops 8336 | bytes 66688 | tf_op jit(solution)/shard_map/psum | solution.py:85
  916.1 0.6 broadcast_multiply_fusion
  916.7 0.8 fusion.1
  917.6 0.6 copy-done.6
  918.2 0.5 sub.23
  918.7 0.5 broadcast_multiply_fusion.1
  919.2 142.4 %all-reduce.9.cloned.1.call-done = bf16[128,512]{0,1:T(8,128)(2,1)} async-done(((bf16[128,512]{0,1:T(8,128)(2,1)}), bf16[128,512]{0,1:T(8,128)(2,1)}) %all-reduce.9.cloned.1.call-update) | async-done | bytes 131088 | tf_op jit(solution)/shard_map/psum | solution.py:82
  1061.7 1.3 convert_subtract_fusion.2
  (71 shorter events, 4.7 us)
Async XLA Ops:
  7.2 7.2 copy-start.2
  76.2 1.1 copy-start.5
  78.4 277.4 %all-to-all-start = ((bf16[32,2,1024]{2,1,0:T(2,128)(2,1)}), bf16[32,2,1024]{2,1,0:T(2,128)(2,1)S(1)}, u32[]{:S(2)}, u32[]{:S(2)}) async-start(bf16[32,2,1024]{2,1,0:T(2,128)(2,1)} %reshape.118), calls=%async_computation | async-start | bytes 262144 | tf_op jit(solution)/shard_map/all_to_all | solution.py:59
  85.7 0.7 copy-start.4
  139.1 46.8 %copy-start.1 = (bf16[3,64,128]{2,1,0:T(8,128)(2,1)S(1)}, bf16[3,64,128]{2,1,0:T(8,128)(2,1)}, u32[]{:S(2)}) copy-start(bf16[3,64,128]{2,1,0:T(8,128)(2,1)} %param.12) | copy-start | bytes 147460
  357.0 64.0 %all-to-all-start.1 = ((bf16[16,128,32]{1,2,0:T(8,128)(2,1)}), bf16[16,128,32]{1,2,0:T(8,128)(2,1)S(1)}, u32[]{:S(2)}, u32[]{:S(2)}) async-start(bf16[16,128,32]{1,2,0:T(8,128)(2,1)} %copy.54), calls=%async_computation.1 | async-start | bytes 262144 | tf_op jit(solution)/shard_map/all_to_all | solution.py:66
  387.7 120.7 %reduce-scatter.7.cloned.1.call-start = ((), (), s32[]{:S(2)}) async-start(), calls=%async_computation.9 | async-start | bytes 278528
  560.9 61.0 %all-to-all-start.2 = ((bf16[32,2,1024]{2,1,0:T(2,128)(2,1)}), bf16[32,2,1024]{2,1,0:T(2,128)(2,1)S(1)}, u32[]{:S(2)}, u32[]{:S(2)}) async-start(bf16[32,2,1024]{2,1,0:T(2,128)(2,1)} %reshape.120), calls=%async_computation.2 | async-start | bytes 262144 | tf_op jit(solution)/shard_map/all_to_all | solution.py:59
  570.7 50.9 %copy-start = (bf16[128,3,128]{2,0,1:T(8,128)(2,1)S(1)}, bf16[128,3,128]{2,0,1:T(8,128)(2,1)}, u32[]{:S(2)}) copy-start(bf16[128,3,128]{2,0,1:T(8,128)(2,1)} %param.13) | copy-start | bytes 294916
  623.1 42.6 %all-to-all-start.3 = ((bf16[16,128,32]{1,2,0:T(8,128)(2,1)}), bf16[16,128,32]{1,2,0:T(8,128)(2,1)S(1)}, u32[]{:S(2)}, u32[]{:S(2)}) async-start(bf16[16,128,32]{1,2,0:T(8,128)(2,1)} %copy.59), calls=%async_computation.3 | async-start | bytes 262144 | tf_op jit(solution)/shard_map/all_to_all | solution.py:66
  658.0 90.0 %reduce-scatter.9.cloned.1.call-start = ((), (), s32[]{:S(2)}) async-start(), calls=%async_computation.10 | async-start | bytes 278528
  800.9 23.2 %all-to-all-start.4 = ((bf16[32,2,1024]{2,1,0:T(2,128)(2,1)}), bf16[32,2,1024]{2,1,0:T(2,128)(2,1)S(1)}, u32[]{:S(2)}, u32[]{:S(2)}) async-start(bf16[32,2,1024]{2,1,0:T(2,128)(2,1)} %reshape.122), calls=%async_computation.4 | async-start | bytes 262144 | tf_op jit(solution)/shard_map/all_to_all | solution.py:59
  825.3 30.2 %all-to-all-start.5 = ((bf16[16,128,32]{1,2,0:T(8,128)(2,1)}), bf16[16,128,32]{1,2,0:T(8,128)(2,1)S(1)}, u32[]{:S(2)}, u32[]{:S(2)}) async-start(bf16[16,128,32]{1,2,0:T(8,128)(2,1)} %copy.65), calls=%async_computation.5 | async-start | bytes 262144 | tf_op jit(solution)/shard_map/all_to_all | solution.py:66
  847.9 213.8 %all-reduce.9.cloned.1.call-start = ((), (), s32[]{:S(2)}) async-start(), calls=%async_computation.8 | async-start | bytes 262144 | tf_op jit(solution)/shard_map/psum | solution.py:82
  917.5 144.1 %copy-start.3 = (bf16[128,32]{0,1:T(8,128)(2,1)S(1)}, bf16[128,32]{0,1:T(8,128)(2,1)}, u32[]{:S(2)}) copy-start(bf16[128,32]{0,1:T(8,128)(2,1)} %param.14) | copy-start | bytes 24580
  917.5 0.7 copy-start.6
Sparse Core Ops, SparseCore 0:
  422.1 86.2 reduce-scatter.6
  667.0 81.0 reduce-scatter.8
  917.7 143.9 all-reduce.8
